TPU v7x, 32 devices: a whole 2x2x4 slice. The times are simulated.
32 devices in a mesh: rep: 2 (over x), dp: 4 (over y, core), ctx: 4 (over z).
Axes of the slice: x: 2, y: 2, z: 4, core: 2. Of those that a mesh axis runs over, the one named last changes fastest.
Arguments:
- frames: bfloat16 [8, 512, 1024], P(('rep', 'dp'), 'ctx'), may hold values from -24 to 24
- lengths: int32 [8], P(('rep', 'dp')), may hold values from 64 to 512, as said below
- cotangent: bfloat16 [8, 512, 1024], P(('rep', 'dp'), 'ctx'), may hold values from -6 to 6
- w_query: bfloat16 [1024, 512], P('dp'), may hold values from -0.5 to 0.5
- w_key: bfloat16 [1024, 512], P('dp'), may hold values from -0.5 to 0.5
- w_value: bfloat16 [1024, 512], P('dp'), may hold values from -0.1875 to 0.1875
- w_out: bfloat16 [512, 1024], P('dp'), may hold values from -0.25 to 0.25
Outputs:
- attended: bfloat16 [8, 512, 1024], P(('rep', 'dp'), 'ctx')
- grad_frames: bfloat16 [8, 512, 1024], P(('rep', 'dp'), 'ctx')
- grad_out: float32 [512, 1024], P('dp')
Inputs may be any that keep to these rules, and one draw needn't show every extreme that they name: `lengths`: number of real frames of each meeting; one meeting of every draw has all 512 frames real.
All inputs are finite; a program needn't handle non-finite values.
Results may differ from a plain program's by a relative error of at most 0.025.
The roundings to bfloat16 on the way count: a program that leaves them out, or rounds other values in their place, can miss the bound.
Values may be sent and summed in bfloat16 or wider, within the bound.
A program may use at most 64 MiB of HBM per device.

v0:
```python
import math
import jax
import jax.numpy as jnp
from jax import lax
from jax.sharding import PartitionSpec as P

HEAD = 128
MASKED_SCORE = -1e30


def head_split(matrix, head_count):
    return matrix.reshape(matrix.shape[0], head_count, matrix.shape[1] // head_count)


def forward_step(carry, key_part, value_part, offset, query_heads, length, score_scale):
    head_count = query_heads.shape[1]
    amount = key_part.shape[0]
    maxima, totals, accumulated = carry
    key_heads = head_split(key_part, head_count)
    value_heads = head_split(value_part, head_count)
    scores = (
        jnp.einsum("rhe,nhe->hrn", query_heads, key_heads, preferred_element_type=jnp.float32)
        * score_scale
    )
    usable = offset + jnp.arange(amount) < length
    scores = jnp.where(usable[None, None, :], scores, MASKED_SCORE)
    new_maxima = jnp.maximum(maxima, jnp.max(scores, axis=2))
    factor = jnp.exp(maxima - new_maxima)
    exponent = jnp.where(usable[None, None, :], jnp.exp(scores - new_maxima[:, :, None]), 0.0)
    totals = totals * factor + jnp.sum(exponent, axis=2)
    mixed = jnp.einsum(
        "hrn,nhe->hre",
        exponent.astype(jnp.bfloat16),
        value_heads,
        preferred_element_type=jnp.float32,
    )
    accumulated = accumulated * factor[:, :, None] + mixed
    return (new_maxima, totals, accumulated)


def query_step(
    grad_accum,
    key_part,
    value_part,
    offset,
    query_heads,
    context_heads,
    logsum,
    deltas,
    length,
    score_scale,
):
    head_count = query_heads.shape[1]
    amount = key_part.shape[0]
    key_heads = head_split(key_part, head_count)
    value_heads = head_split(value_part, head_count)
    scores = (
        jnp.einsum("rhe,nhe->hrn", query_heads, key_heads, preferred_element_type=jnp.float32)
        * score_scale
    )
    usable = offset + jnp.arange(amount) < length
    attention = jnp.where(usable[None, None, :], jnp.exp(scores - logsum[:, :, None]), 0.0)
    grad_prob = jnp.einsum(
        "rhe,nhe->hrn", context_heads, value_heads, preferred_element_type=jnp.float32
    )
    grad_score = (attention * (grad_prob - deltas[:, :, None])).astype(jnp.bfloat16)
    added = jnp.einsum("hrn,nhe->rhe", grad_score, key_heads, preferred_element_type=jnp.float32)
    return grad_accum + added * score_scale


def key_step(
    query_part,
    context_part,
    all_logsum,
    all_deltas,
    key_heads,
    value_heads,
    key_usable,
    score_scale,
):
    head_count = key_heads.shape[1]
    query_heads = head_split(query_part, head_count)
    context_heads = head_split(context_part, head_count)
    scores = (
        jnp.einsum("rhe,nhe->hrn", query_heads, key_heads, preferred_element_type=jnp.float32)
        * score_scale
    )
    attention = jnp.where(key_usable[None, None, :], jnp.exp(scores - all_logsum[:, :, None]), 0.0)
    grad_value = jnp.einsum(
        "hrn,rhe->nhe",
        attention.astype(jnp.bfloat16),
        context_heads,
        preferred_element_type=jnp.float32,
    )
    grad_prob = jnp.einsum(
        "rhe,nhe->hrn", context_heads, value_heads, preferred_element_type=jnp.float32
    )
    grad_score = (attention * (grad_prob - all_deltas[:, :, None])).astype(jnp.bfloat16)
    added = jnp.einsum("hrn,rhe->nhe", grad_score, query_heads, preferred_element_type=jnp.float32)
    return (added * score_scale, grad_value)


def back_project(gradient, weight):
    return lax.dot_general(
        gradient, weight, (((1,), (1,)), ((), ())), preferred_element_type=jnp.float32
    )


def shards(frames, lengths, cotangent, w_query, w_key, w_value, w_out):
    full_query, full_key, full_value, full_out = (
        lax.all_gather(w_query, "dp", axis=0, tiled=True),
        lax.all_gather(w_key, "dp", axis=0, tiled=True),
        lax.all_gather(w_value, "dp", axis=0, tiled=True),
        lax.all_gather(w_out, "dp", axis=0, tiled=True),
    )
    inputs = frames[0]
    upstream = cotangent[0]
    length = lengths[0]
    row_count = inputs.shape[0]
    inner_width = full_query.shape[1]
    head_count = inner_width // HEAD
    score_scale = HEAD ** (-0.5)
    first_frame = lax.axis_index("ctx") * row_count
    row_usable = first_frame + jnp.arange(row_count) < length
    queries = jnp.dot(inputs, full_query, preferred_element_type=jnp.float32).astype(jnp.bfloat16)
    keys = jnp.dot(inputs, full_key, preferred_element_type=jnp.float32).astype(jnp.bfloat16)
    values = jnp.dot(inputs, full_value, preferred_element_type=jnp.float32).astype(jnp.bfloat16)
    query_heads = head_split(queries, head_count)
    key_heads = head_split(keys, head_count)
    value_heads = head_split(values, head_count)
    start_state = (
        jnp.full((head_count, row_count), MASKED_SCORE, jnp.float32),
        jnp.zeros((head_count, row_count), jnp.float32),
        jnp.zeros((head_count, row_count, HEAD), jnp.float32),
    )
    all_keys, all_values = (
        lax.all_gather(keys, "ctx", axis=0, tiled=True),
        lax.all_gather(values, "ctx", axis=0, tiled=True),
    )
    key_block = row_count * math.gcd(max(1, 512 // row_count), lax.axis_size("ctx"))
    block_count = all_keys.shape[0] // key_block
    key_blocks = all_keys.reshape(block_count, key_block, inner_width)
    value_blocks = all_values.reshape(block_count, key_block, inner_width)
    block_starts = jnp.arange(block_count, dtype=jnp.int32) * key_block

    def scan_forward(current, scan_item):
        return (
            forward_step(
                current, scan_item[0], scan_item[1], scan_item[2], query_heads, length, score_scale
            ),
            None,
        )

    softmax_state, unused = lax.scan(
        scan_forward, start_state, (key_blocks, value_blocks, block_starts)
    )
    maxima, totals, accumulated = softmax_state
    context = (
        (accumulated / totals[:, :, None])
        .transpose(1, 0, 2)
        .reshape(row_count, inner_width)
        .astype(jnp.bfloat16)
    )
    logsum = maxima + jnp.log(totals)
    attended = jnp.dot(context, full_out, preferred_element_type=jnp.float32)
    attended = jnp.where(row_usable[:, None], attended, 0.0).astype(jnp.bfloat16)
    masked_grad = jnp.where(row_usable[:, None], upstream, jnp.zeros_like(upstream))
    grad_context = back_project(masked_grad, full_out).astype(jnp.bfloat16)
    deltas = jnp.sum(
        (grad_context.astype(jnp.float32) * context.astype(jnp.float32)).reshape(
            row_count, head_count, HEAD
        ),
        axis=2,
    )
    context_heads = head_split(grad_context, head_count)
    delta_heads = deltas.T
    all_logsum, all_deltas = (
        lax.all_gather(logsum, "ctx", axis=1, tiled=True),
        lax.all_gather(delta_heads, "ctx", axis=1, tiled=True),
    )
    zero_grad = jnp.zeros((row_count, head_count, HEAD), jnp.float32)

    def scan_query(current, scan_item):
        return (
            query_step(
                current,
                scan_item[0],
                scan_item[1],
                scan_item[2],
                query_heads,
                context_heads,
                logsum,
                delta_heads,
                length,
                score_scale,
            ),
            None,
        )

    grad_query, unused = lax.scan(scan_query, zero_grad, (key_blocks, value_blocks, block_starts))
    grad_key, grad_value = key_step(
        lax.all_gather(queries, "ctx", axis=0, tiled=True),
        lax.all_gather(grad_context, "ctx", axis=0, tiled=True),
        all_logsum,
        all_deltas,
        key_heads,
        value_heads,
        row_usable,
        score_scale,
    )
    grad_query = grad_query.reshape(row_count, inner_width).astype(jnp.bfloat16)
    grad_key = grad_key.reshape(row_count, inner_width).astype(jnp.bfloat16)
    grad_value = grad_value.reshape(row_count, inner_width).astype(jnp.bfloat16)
    grad_input = (
        back_project(grad_query, full_query)
        + back_project(grad_key, full_key)
        + back_project(grad_value, full_value)
    )
    grad_frames = grad_input.astype(jnp.bfloat16)
    summed_grad = lax.psum(
        lax.dot_general(
            context, masked_grad, (((0,), (0,)), ((), ())), preferred_element_type=jnp.float32
        ),
        ("rep", "ctx"),
    )
    grad_out = lax.psum_scatter(summed_grad, "dp", scatter_dimension=0, tiled=True)
    return (attended[None], grad_frames[None], grad_out)


def solution(mesh):
    in_specs = (
        P(("rep", "dp"), "ctx", None),
        P(("rep", "dp")),
        P(("rep", "dp"), "ctx", None),
        P("dp", None),
        P("dp", None),
        P("dp", None),
        P("dp", None),
    )
    out_specs = (P(("rep", "dp"), "ctx", None), P(("rep", "dp"), "ctx", None), P("dp", None))
    return jax.shard_map(shards, mesh=mesh, in_specs=in_specs, out_specs=out_specs, check_vma=False)
```

profile of v0, /device:TPU:0, one launch (start us, length us, event | category | flops | bytes accessed | tf_op | source)
XLA Modules:
  0.0 236.2 jit_solution(8206433220303085801)
XLA Ops:
  7.2 0.7 all-gather.9.cloned.1.call-update
  7.9 0.0 all-gather.7.cloned.1.call-start
  8.0 0.7 all-gather.7.cloned.1.call-update
  8.7 0.0 all-gather.5.cloned.1.call-start
  8.7 0.7 all-gather.5.cloned.1.call-update
  9.4 0.0 all-gather.11.cloned.1.call-start
  9.4 0.5 all-gather.11.cloned.1.call-update
  10.0 0.0 reduce-scatter.2.cloned.1.call-start
  10.7 18.3 %all-gather.9.cloned.1.call-done = bf16[1024,512]{1,0:T(8,128)(2,1)} async-done(((bf16[256,512]{1,0:T(8,128)(2,1)}), bf16[1024,512]{1,0:T(8,128)(2,1)}) %all-gather.9.cloned.1.call-update) | async-done | bytes 1048592 | tf_op jit(solution)/shard_map/all_gather | solution.py:113
  29.0 1.5 convolution_convert_fusion.2
  30.6 16.1 %all_gather.34 = bf16[512,512]{1,0:T(8,128)(2,1)S(1)} all-gather(bf16[128,512]{1,0:T(8,128)(2,1)S(1)} %convolution_convert_fusion.2), channel_id=1, replica_groups=mesh['rep'=2,'dp'=4,'ctx'=4] {'ctx'}, dimensions={0}, use_global_device_ids=true | all-gather | bytes 655360 | tf_op jit(solution)/shard_map/all_gather | solution.py:138
  46.6 0.2 copy.33
  46.9 0.5 all-gather.7.cloned.1.call-done
  47.4 1.5 convolution_convert_fusion.3
  48.9 16.0 %all_gather.32 = bf16[512,512]{1,0:T(8,128)(2,1)S(1)} all-gather(bf16[128,512]{1,0:T(8,128)(2,1)S(1)} %convolution_convert_fusion.3), channel_id=1, replica_groups=mesh['rep'=2,'dp'=4,'ctx'=4] {'ctx'}, dimensions={0}, use_global_device_ids=true | all-gather | bytes 655360 | tf_op jit(solution)/shard_map/all_gather | solution.py:137
  64.9 0.2 copy.35
  65.1 0.5 all-gather.5.cloned.1.call-done
  65.7 1.5 convolution_convert_fusion.4
  67.2 0.4 select_reduce_fusion
  67.6 0.3 fusion.23
  68.0 0.4 fusion.19
  68.4 0.2 copy-done.5
  68.6 1.8 fusion.36
  70.4 0.0 all-reduce.2.cloned.1.call-start
  70.5 0.1 copy.22
  70.6 0.8 copy.34
  71.3 12.5 %all-gather.11.cloned.1.call-done = bf16[512,1024]{1,0:T(8,128)(2,1)} async-done(((bf16[128,1024]{1,0:T(8,128)(2,1)}), bf16[512,1024]{1,0:T(8,128)(2,1)}) %all-gather.11.cloned.1.call-update) | async-done | bytes 1048592 | tf_op jit(solution)/shard_map/all_gather | solution.py:114
  83.9 1.7 convert_multiply_fusion
  85.6 0.1 reshape.104
  85.7 0.2 reduce_sum.23
  85.9 0.6 copy.23
  86.5 16.1 %all_gather.36 = bf16[512,512]{1,0:T(8,128)(2,1)S(1)} all-gather(bf16[128,512]{1,0:T(8,128)(2,1)S(1)} %convolution_convert_fusion.4), channel_id=1, replica_groups=mesh['rep'=2,'dp'=4,'ctx'=4] {'ctx'}, dimensions={0}, use_global_device_ids=true | all-gather | bytes 655360 | tf_op jit(solution)/shard_map/all_gather | solution.py:202
  102.6 1.1 copy.36
  103.6 16.0 %all_gather.38 = bf16[512,512]{1,0:T(8,128)(2,1)S(1)} all-gather(bf16[128,512]{1,0:T(8,128)(2,1)S(1)} %get-tuple-element.50), channel_id=1, replica_groups=mesh['rep'=2,'dp'=4,'ctx'=4] {'ctx'}, dimensions={0}, use_global_device_ids=true | all-gather | bytes 655360 | tf_op jit(solution)/shard_map/all_gather | solution.py:203
  119.6 0.2 copy.37
  119.8 14.3 %all_gather.39 = f32[4,512]{0,1:T(8,128)S(1)} all-gather(f32[4,128]{0,1:T(8,128)S(1)} %bitcast.109), channel_id=1, replica_groups=mesh['rep'=2,'dp'=4,'ctx'=4] {'ctx'}, dimensions={1}, use_global_device_ids=true | all-gather | bytes 10240 | tf_op jit(solution)/shard_map/all_gather | solution.py:179
  134.1 0.1 copy.27
  134.2 11.9 %all_gather.37 = f32[4,512]{1,0:T(4,128)S(1)} all-gather(f32[4,128]{1,0:T(4,128)S(1)} %get-tuple-element.36), channel_id=1, replica_groups=mesh['rep'=2,'dp'=4,'ctx'=4] {'ctx'}, dimensions={1}, use_global_device_ids=true | all-gather | bytes 10240 | tf_op jit(solution)/shard_map/all_gather | solution.py:178
  146.1 1.6 fusion.3
  147.6 1.0 convolution_convert_fusion
  148.7 2.3 fusion.18
  151.0 2.7 %fusion.60 = f32[128,1024]{1,0:T(8,128)} fusion(bf16[128,512]{0,1:T(8,128)(2,1)} %bitcast.115, bf16[1024,512]{1,0:T(8,128)(2,1)} %all-gather.5.cloned.1.call-done), kind=kOutput, calls=%fused_computation.80 | convolution fusion | flops 134217728 | bytes 1703936 | tf_op jit(solution)/shard_map/dot_general | solution.py:104
  153.7 2.9 %fusion.17 = bf16[4,128,128]{2,1,0:T(8,128)(2,1)} fusion(bf16[512,4,128]{0,2,1:T(8,128)(2,1)} %bitcast.104, f32[4,512,128]{2,1,0:T(8,128)} %copy-done.4, bf16[512,4,128]{0,2,1:T(8,128)(2,1)S(1)} %bitcast.100, bf16[128,4,128]{0,2,1:T(8,128)(2,1)} %bitcast.111, f32[4,512]{1,0:T(4,128)S(1)} %copy.27), kind=kOutput, calls=%fused_computation.30 | convolution fusion | flops 135135232 | bytes 2367488 | tf_op jit(solution)/shard_map/hrn,rhe->nhe/dot_general | solution.py:99
  156.6 1.0 fusion.14
  157.6 1.6 convolution_add_fusion.1
  159.3 1.2 fusion.13
  160.4 67.1 %all-reduce.2.cloned.1.call-done = f32[128,1024]{1,0:T(8,128)} async-done(((f32[128,1024]{1,0:T(8,128)}), f32[128,1024]{1,0:T(8,128)}) %all-reduce.2.cloned.1.call-update) | async-done | bytes 524304 | tf_op jit(solution)/shard_map/psum | solution.py:220
  227.5 1.9 copy.58
  (30 shorter events, 0.2 us)
Async XLA Ops:
  7.2 21.9 %copy-start = (bf16[1,128,1024]{2,1,0:T(8,128)(2,1)S(1)}, bf16[1,128,1024]{2,1,0:T(8,128)(2,1)}, u32[]{:S(2)}) copy-start(bf16[1,128,1024]{2,1,0:T(8,128)(2,1)} %param.7) | copy-start | bytes 786436
  7.2 21.9 %all-gather.9.cloned.1.call-start = ((), (), s32[]{:S(2)}) async-start(), calls=%async_computation.3 | async-start | bytes 1310720 | tf_op jit(solution)/shard_map/all_gather | solution.py:113
  7.9 39.4 %all-gather.7.cloned.1.call-start = ((), (), s32[]{:S(2)}) async-start(), calls=%async_computation.2 | async-start | bytes 1310720 | tf_op jit(solution)/shard_map/all_gather | solution.py:112
  8.7 57.0 %all-gather.5.cloned.1.call-start = ((), (), s32[]{:S(2)}) async-start(), calls=%async_computation.1 | async-start | bytes 1310720 | tf_op jit(solution)/shard_map/all_gather | solution.py:111
  9.4 74.5 %all-gather.11.cloned.1.call-start = ((), (), s32[]{:S(2)}) async-start(), calls=%async_computation.4 | async-start | bytes 1310720 | tf_op jit(solution)/shard_map/all_gather | solution.py:114
  10.0 146.6 %reduce-scatter.2.cloned.1.call-start = ((), (), s32[]{:S(2)}) async-start(), calls=%async_computation.5 | async-start | bytes 2621440 | tf_op jit(solution)/shard_map/reduce_scatter | solution.py:226
  10.7 57.3 %copy-start.10 = (pred[512]{0:T(512)(128)(4,1)}, pred[512]{0:T(512)(128)(4,1)S(1)}, u32[]{:S(2)}) copy-start(pred[512]{0:T(512)(128)(4,1)S(1)} %iota_compare_fusion) | copy-start | bytes 1540
  46.9 21.1 %copy-start.6 = (bf16[512,512]{0,1:T(8,128)(2,1)}, bf16[512,512]{0,1:T(8,128)(2,1)S(1)}, u32[]{:S(2)}) copy-start(bf16[512,512]{0,1:T(8,128)(2,1)S(1)} %copy.33) | copy-start | bytes 1572868
  48.9 18.3 %copy-start.7 = (bf16[128,512]{1,0:T(8,128)(2,1)}, bf16[128,512]{1,0:T(8,128)(2,1)S(1)}, u32[]{:S(2)}) copy-start(bf16[128,512]{1,0:T(8,128)(2,1)S(1)} %convolution_convert_fusion.3) | copy-start | bytes 393220
  67.6 1.0 copy-start.5
  70.4 157.1 %all-reduce.2.cloned.1.call-start = ((), (), s32[]{:S(2)}) async-start(), calls=%async_computation.6 | async-start | bytes 1048576 | tf_op jit(solution)/shard_map/psum | solution.py:220
  85.6 34.3 %copy-start.8 = (bf16[128,512]{1,0:T(8,128)(2,1)}, bf16[128,512]{1,0:T(8,128)(2,1)S(1)}, u32[]{:S(2)}) copy-start(bf16[128,512]{1,0:T(8,128)(2,1)S(1)} %get-tuple-element.50) | copy-start | bytes 393220
  147.6 3.4 %copy-start.4 = (f32[4,512,128]{2,1,0:T(8,128)}, f32[4,512,128]{2,1,0:T(8,128)S(1)}, u32[]{:S(2)}) copy-start(f32[4,512,128]{2,1,0:T(8,128)S(1)} %fusion.3) | copy-start | bytes 3145732
  151.0 5.6 %copy-start.2 = (bf16[512,1024]{1,0:T(8,128)(2,1)S(1)}, bf16[512,1024]{1,0:T(8,128)(2,1)}, u32[]{:S(2)}) copy-start(bf16[512,1024]{1,0:T(8,128)(2,1)} %all-gather.11.cloned.1.call-done) | copy-start | bytes 3145732
  153.7 4.0 %copy-start.1 = (bf16[1024,512]{1,0:T(8,128)(2,1)S(1)}, bf16[1024,512]{1,0:T(8,128)(2,1)}, u32[]{:S(2)}) copy-start(bf16[1024,512]{1,0:T(8,128)(2,1)} %all-gather.7.cloned.1.call-done) | copy-start | bytes 3145732
  156.6 2.7 %copy-start.3 = (bf16[1024,512]{1,0:T(8,128)(2,1)S(1)}, bf16[1024,512]{1,0:T(8,128)(2,1)}, u32[]{:S(2)}) copy-start(bf16[1024,512]{1,0:T(8,128)(2,1)} %all-gather.9.cloned.1.call-done) | copy-start | bytes 3145732
  156.6 2.7 %copy-start.9 = (bf16[4,128,128]{2,1,0:T(8,128)(2,1)S(1)}, bf16[4,128,128]{2,1,0:T(8,128)(2,1)}, u32[]{:S(2)}) copy-start(bf16[4,128,128]{2,1,0:T(8,128)(2,1)} %convolution_convert_fusion) | copy-start | bytes 393220
Sparse Core Ops, SparseCore 0:
  9.6 19.4 all-gather.8
  30.6 16.7 all-gather.6
  48.9 16.7 all-gather.4
  67.1 16.7 all-gather.10
  86.2 31.4 reduce-scatter.1
  156.7 70.7 all-reduce.1
where the time goes:
time: 237 us; the launch traced here: 236 us
  waiting for transfers between devices  102 us (43%)
  blocking collectives  90.2 us (38%)
  matrix products  23.2 us (10%)
  between operations  15 us (6%)
  local copies, waits for them, and re-layouts  5.47 us (2%)
    psum x1, waiting for transfers between devices, shards(): lax.psum(lax.dot_general(context, masked_grad, (((0,), (0,)), ((), ())),...  67.1 us
    all_gather x1, waiting for transfers between devices, shards(): lax.all_gather(w_value, 'dp', axis=0, tiled=True)  18.3 us
    all_gather x1, blocking collectives, shards(): lax.all_gather(values, 'ctx', axis=0, tiled=True)  16.1 us
    all_gather x1, blocking collectives, shards(): lax.all_gather(queries, 'ctx', axis=0, tiled=True)  16.1 us
    all_gather x1, blocking collectives, shards(): lax.all_gather(keys, 'ctx', axis=0, tiled=True)  16 us
    all_gather x1, blocking collectives, shards(): lax.all_gather(grad_context, 'ctx', axis=0, tiled=True)  16 us
    all_gather x1, blocking collectives, shards(): lax.all_gather(delta_heads, 'ctx', axis=1, tiled=True)  14.3 us
    all_gather x1, waiting for transfers between devices, shards(): lax.all_gather(w_out, 'dp', axis=0, tiled=True)  12.5 us
  transfers between devices with their start and end apart: 6, of which 5 were waited for; matrix products, arithmetic and copies ran while one was open for 11% of the time, Pallas kernels for 0%

commit v1 on v0

--- a/solution.py
+++ b/solution.py
@@ -218,10 +218,13 @@
     )
     grad_frames = grad_input.astype(jnp.bfloat16)
     summed_grad = lax.psum(
-        lax.dot_general(
-            context, masked_grad, (((0,), (0,)), ((), ())), preferred_element_type=jnp.float32
+        lax.psum(
+            lax.dot_general(
+                context, masked_grad, (((0,), (0,)), ((), ())), preferred_element_type=jnp.float32
+            ),
+            "ctx",
         ),
-        ("rep", "ctx"),
+        "rep",
     )
     grad_out = lax.psum_scatter(summed_grad, "dp", scatter_dimension=0, tiled=True)
     return (attended[None], grad_frames[None], grad_out)

time: 237 us -> 230 us (0.970)
  waiting for transfers between devices: 102 us -> 93.8 us
    psum x1, waiting for transfers between devices: 67.1 us -> 32 us  [shards(): lax.psum(lax.dot_general(context, masked_grad, (((0,), (0,)), ((), ())),...]
    psum x0 -> x1, waiting for transfers between devices: none -> 27.3 us  [shards(): lax.psum(lax.psum(lax.dot_general(context, masked_grad, (((0,), (0,)), ((...]
  transfers between devices with their start and end apart: 6 -> 7, of which waited for: 5 -> 6; matrix products, arithmetic and copies ran while one was open for 11% -> 11% of each run, Pallas kernels for 0% -> 0%
where the time goes in v1:
time: 230 us; the launch traced here: 229 us
  waiting for transfers between devices  93.8 us (41%)
  blocking collectives  90.8 us (39%)
  matrix products  22.4 us (10%)
  between operations  15 us (7%)
  local copies, waits for them, and re-layouts  6.23 us (3%)
    psum x1, waiting for transfers between devices, shards(): lax.psum(lax.dot_general(context, masked_grad, (((0,), (0,)), ((), ())),...  32 us
    psum x1, waiting for transfers between devices, shards(): lax.psum(lax.psum(lax.dot_general(context, masked_grad, (((0,), (0,)), ((...  27.3 us
    all_gather x1, waiting for transfers between devices, shards(): lax.all_gather(w_value, 'dp', axis=0, tiled=True)  18.3 us
    all_gather x1, blocking collectives, shards(): lax.all_gather(grad_context, 'ctx', axis=0, tiled=True)  16.2 us
    all_gather x1, blocking collectives, shards(): lax.all_gather(values, 'ctx', axis=0, tiled=True)  16.1 us
    all_gather x1, blocking collectives, shards(): lax.all_gather(queries, 'ctx', axis=0, tiled=True)  16.1 us
    all_gather x1, blocking collectives, shards(): lax.all_gather(keys, 'ctx', axis=0, tiled=True)  16 us
    all_gather x1, blocking collectives, shards(): lax.all_gather(delta_heads, 'ctx', axis=1, tiled=True)  14.5 us
  transfers between devices with their start and end apart: 7, of which 6 were waited for; matrix products, arithmetic and copies ran while one was open for 11% of the time, Pallas kernels for 0%

profile of v1, /device:TPU:0, one launch (start us, length us, event | category | flops | bytes accessed | tf_op | source)
XLA Modules:
  0.0 229.2 jit_solution(3642026689041059304)
XLA Ops:
  7.2 0.7 all-gather.9.cloned.1.call-update
  8.0 0.7 all-gather.7.cloned.1.call-update
  8.7 0.7 all-gather.5.cloned.1.call-update
  9.4 0.5 all-gather.11.cloned.1.call-update
  10.0 0.0 reduce-scatter.2.cloned.1.call-start
  10.7 18.3 %all-gather.9.cloned.1.call-done = bf16[1024,512]{1,0:T(8,128)(2,1)} async-done(((bf16[256,512]{1,0:T(8,128)(2,1)}), bf16[1024,512]{1,0:T(8,128)(2,1)}) %all-gather.9.cloned.1.call-update) | async-done | bytes 1048592 | tf_op jit(solution)/shard_map/all_gather | solution.py:113
  29.0 1.5 convolution_convert_fusion.2
  30.6 16.1 %all_gather.34 = bf16[512,512]{1,0:T(8,128)(2,1)S(1)} all-gather(bf16[128,512]{1,0:T(8,128)(2,1)S(1)} %convolution_convert_fusion.2), channel_id=1, replica_groups=mesh['rep'=2,'dp'=4,'ctx'=4] {'ctx'}, dimensions={0}, use_global_device_ids=true | all-gather | bytes 655360 | tf_op jit(solution)/shard_map/all_gather | solution.py:138
  46.6 0.2 copy.33
  46.9 0.5 all-gather.7.cloned.1.call-done
  47.4 1.5 convolution_convert_fusion.3
  48.9 16.0 %all_gather.32 = bf16[512,512]{1,0:T(8,128)(2,1)S(1)} all-gather(bf16[128,512]{1,0:T(8,128)(2,1)S(1)} %convolution_convert_fusion.3), channel_id=1, replica_groups=mesh['rep'=2,'dp'=4,'ctx'=4] {'ctx'}, dimensions={0}, use_global_device_ids=true | all-gather | bytes 655360 | tf_op jit(solution)/shard_map/all_gather | solution.py:137
  64.9 0.2 copy.35
  65.1 0.5 all-gather.5.cloned.1.call-done
  65.7 1.5 convolution_convert_fusion.4
  67.2 0.4 select_reduce_fusion
  67.6 0.3 fusion.23
  68.0 0.4 fusion.19
  68.4 0.2 copy-done.6
  68.6 1.8 fusion.36
  70.4 0.0 all-reduce.5.cloned.1.call-start
  70.5 0.1 copy.22
  70.6 0.8 copy.34
  71.3 12.5 %all-gather.11.cloned.1.call-done = bf16[512,1024]{1,0:T(8,128)(2,1)} async-done(((bf16[128,1024]{1,0:T(8,128)(2,1)}), bf16[512,1024]{1,0:T(8,128)(2,1)}) %all-gather.11.cloned.1.call-update) | async-done | bytes 1048592 | tf_op jit(solution)/shard_map/all_gather | solution.py:114
  83.9 2.4 %convert_multiply_fusion = (f32[128,512]{1,0:T(8,128)S(1)}, bf16[128,512]{1,0:T(8,128)(2,1)}) fusion(bf16[128,512]{1,0:T(8,128)(2,1)S(1)} %copy.22, bf16[512,1024]{1,0:T(8,128)(2,1)} %all-gather.11.cloned.1.call-done, bf16[1,128,1024]{2,1,0:T(8,128)(2,1)S(1)} %copy-done.6, pred[128]{0:T(512)(128)(4,1)S(1)} %add_compare_fusion), kind=kOutput, calls=%fused_computation.57 | convolution fusion | flops 134610944 | bytes 1835136 | tf_op jit(solution)/shard_map/dot_general | solution.py:104
  86.2 0.1 reshape.104
  86.3 0.2 reduce_sum.23
  86.5 0.6 copy-done.7
  87.1 0.6 copy.23
  87.8 16.1 %all_gather.36 = bf16[512,512]{1,0:T(8,128)(2,1)S(1)} all-gather(bf16[128,512]{1,0:T(8,128)(2,1)S(1)} %convolution_convert_fusion.4), channel_id=1, replica_groups=mesh['rep'=2,'dp'=4,'ctx'=4] {'ctx'}, dimensions={0}, use_global_device_ids=true | all-gather | bytes 655360 | tf_op jit(solution)/shard_map/all_gather | solution.py:202
  103.8 0.2 copy.36
  104.1 16.2 %all_gather.38 = bf16[512,512]{1,0:T(8,128)(2,1)S(1)} all-gather(bf16[128,512]{1,0:T(8,128)(2,1)} %get-tuple-element.50), channel_id=1, replica_groups=mesh['rep'=2,'dp'=4,'ctx'=4] {'ctx'}, dimensions={0}, use_global_device_ids=true | all-gather | bytes 655360 | tf_op jit(solution)/shard_map/all_gather | solution.py:203
  120.3 0.2 copy.37
  120.5 14.5 %all_gather.39 = f32[4,512]{0,1:T(8,128)S(1)} all-gather(f32[4,128]{0,1:T(8,128)} %bitcast.109), channel_id=1, replica_groups=mesh['rep'=2,'dp'=4,'ctx'=4] {'ctx'}, dimensions={1}, use_global_device_ids=true | all-gather | bytes 10240 | tf_op jit(solution)/shard_map/all_gather | solution.py:179
  135.0 0.1 copy.27
  135.1 12.0 %all_gather.37 = f32[4,512]{1,0:T(4,128)S(1)} all-gather(f32[4,128]{1,0:T(4,128)S(1)} %get-tuple-element.36), channel_id=1, replica_groups=mesh['rep'=2,'dp'=4,'ctx'=4] {'ctx'}, dimensions={1}, use_global_device_ids=true | all-gather | bytes 10240 | tf_op jit(solution)/shard_map/all_gather | solution.py:178
  147.1 1.4 fusion.3
  148.5 1.0 copy-done.4
  149.5 0.9 convolution_convert_fusion
  150.4 2.2 fusion.18
  152.7 1.8 fusion.60
  154.5 2.9 %fusion.17 = bf16[4,128,128]{2,1,0:T(8,128)(2,1)} fusion(bf16[512,4,128]{0,2,1:T(8,128)(2,1)} %bitcast.104, f32[4,512,128]{2,1,0:T(8,128)} %copy-done.4, bf16[512,4,128]{0,2,1:T(8,128)(2,1)S(1)} %bitcast.100, bf16[128,4,128]{0,2,1:T(8,128)(2,1)} %bitcast.111, f32[4,512]{1,0:T(4,128)S(1)} %copy.27), kind=kOutput, calls=%fused_computation.30 | convolution fusion | flops 135135232 | bytes 2367488 | tf_op jit(solution)/shard_map/hrn,rhe->nhe/dot_general | solution.py:99
  157.4 32.0 %all-reduce.5.cloned.1.call-done = f32[128,1024]{1,0:T(8,128)} async-done(((f32[128,1024]{1,0:T(8,128)}), f32[128,1024]{1,0:T(8,128)}) %all-reduce.5.cloned.1.call-update) | async-done | bytes 524304 | tf_op jit(solution)/shard_map/psum | solution.py:221
  189.5 1.0 fusion.14
  190.5 1.4 convolution_add_fusion.1
  192.0 1.2 fusion.13
  193.1 27.3 %all-reduce.3.cloned.1.call-done = f32[128,1024]{1,0:T(8,128)} async-done(((f32[128,1024]{1,0:T(8,128)}), f32[128,1024]{1,0:T(8,128)}) %all-reduce.3.cloned.1.call-update) | async-done | bytes 524304 | tf_op jit(solution)/shard_map/psum | solution.py:220
  220.5 1.9 copy.59
  (37 shorter events, 0.3 us)
Async XLA Ops:
  7.2 21.9 %copy-start = (bf16[1,128,1024]{2,1,0:T(8,128)(2,1)S(1)}, bf16[1,128,1024]{2,1,0:T(8,128)(2,1)}, u32[]{:S(2)}) copy-start(bf16[1,128,1024]{2,1,0:T(8,128)(2,1)} %param.7) | copy-start | bytes 786436
  7.2 21.9 %all-gather.9.cloned.1.call-start = ((), (), s32[]{:S(2)}) async-start(), calls=%async_computation.3 | async-start | bytes 1310720 | tf_op jit(solution)/shard_map/all_gather | solution.py:113
  7.9 39.4 %all-gather.7.cloned.1.call-start = ((), (), s32[]{:S(2)}) async-start(), calls=%async_computation.2 | async-start | bytes 1310720 | tf_op jit(solution)/shard_map/all_gather | solution.py:112
  8.7 57.0 %all-gather.5.cloned.1.call-start = ((), (), s32[]{:S(2)}) async-start(), calls=%async_computation.1 | async-start | bytes 1310720 | tf_op jit(solution)/shard_map/all_gather | solution.py:111
  9.4 74.5 %all-gather.11.cloned.1.call-start = ((), (), s32[]{:S(2)}) async-start(), calls=%async_computation.4 | async-start | bytes 1310720 | tf_op jit(solution)/shard_map/all_gather | solution.py:114
  10.0 142.6 %reduce-scatter.2.cloned.1.call-start = ((), (), s32[]{:S(2)}) async-start(), calls=%async_computation.6 | async-start | bytes 2621440 | tf_op jit(solution)/shard_map/reduce_scatter | solution.py:229
  10.7 57.3 %copy-start.12 = (pred[512]{0:T(512)(128)(4,1)}, pred[512]{0:T(512)(128)(4,1)S(1)}, u32[]{:S(2)}) copy-start(pred[512]{0:T(512)(128)(4,1)S(1)} %iota_compare_fusion) | copy-start | bytes 1540
  46.9 21.1 %copy-start.8 = (bf16[512,512]{0,1:T(8,128)(2,1)}, bf16[512,512]{0,1:T(8,128)(2,1)S(1)}, u32[]{:S(2)}) copy-start(bf16[512,512]{0,1:T(8,128)(2,1)S(1)} %copy.33) | copy-start | bytes 1572868
  48.9 18.3 %copy-start.10 = (bf16[128,512]{1,0:T(8,128)(2,1)}, bf16[128,512]{1,0:T(8,128)(2,1)S(1)}, u32[]{:S(2)}) copy-start(bf16[128,512]{1,0:T(8,128)(2,1)S(1)} %convolution_convert_fusion.3) | copy-start | bytes 393220
  67.6 1.0 copy-start.6
  70.4 119.0 %all-reduce.5.cloned.1.call-start = ((), (), s32[]{:S(2)}) async-start(), calls=%async_computation.7 | async-start | bytes 1048576 | tf_op jit(solution)/shard_map/psum | solution.py:221
  86.5 0.6 copy-start.7
  104.1 46.3 %copy-start.5 = (bf16[512,512]{0,1:T(8,128)(2,1)}, bf16[512,512]{0,1:T(8,128)(2,1)S(1)}, u32[]{:S(2)}) copy-start(bf16[512,512]{0,1:T(8,128)(2,1)S(1)} %copy.36) | copy-start | bytes 1572868
  135.1 15.3 %copy-start.9 = (bf16[512,512]{0,1:T(8,128)(2,1)S(1)}, bf16[512,512]{0,1:T(8,128)(2,1)}, u32[]{:S(2)}) copy-start(bf16[512,512]{0,1:T(8,128)(2,1)} %copy-done.8) | copy-start | bytes 1572868
  148.5 1.0 copy-start.4
  152.6 67.8 %all-reduce.3.cloned.1.call-start = ((), (), s32[]{:S(2)}) async-start(), calls=%async_computation.5 | async-start | bytes 1048576 | tf_op jit(solution)/shard_map/psum | solution.py:220
  152.7 36.8 %copy-start.2 = (bf16[512,1024]{1,0:T(8,128)(2,1)S(1)}, bf16[512,1024]{1,0:T(8,128)(2,1)}, u32[]{:S(2)}) copy-start(bf16[512,1024]{1,0:T(8,128)(2,1)} %all-gather.11.cloned.1.call-done) | copy-start | bytes 3145732
  154.5 36.0 %copy-start.1 = (bf16[1024,512]{1,0:T(8,128)(2,1)S(1)}, bf16[1024,512]{1,0:T(8,128)(2,1)}, u32[]{:S(2)}) copy-start(bf16[1024,512]{1,0:T(8,128)(2,1)} %all-gather.7.cloned.1.call-done) | copy-start | bytes 3145732
  189.5 2.5 %copy-start.3 = (bf16[1024,512]{1,0:T(8,128)(2,1)S(1)}, bf16[1024,512]{1,0:T(8,128)(2,1)}, u32[]{:S(2)}) copy-start(bf16[1024,512]{1,0:T(8,128)(2,1)} %all-gather.9.cloned.1.call-done) | copy-start | bytes 3145732
  189.5 2.5 %copy-start.11 = (bf16[4,128,128]{2,1,0:T(8,128)(2,1)S(1)}, bf16[4,128,128]{2,1,0:T(8,128)(2,1)}, u32[]{:S(2)}) copy-start(bf16[4,128,128]{2,1,0:T(8,128)(2,1)} %convolution_convert_fusion) | copy-start | bytes 393220
Sparse Core Ops, SparseCore 0:
  9.6 19.4 all-gather.8
  30.6 16.7 all-gather.6
  48.9 16.7 all-gather.4
  67.1 16.7 all-gather.10
  86.2 31.4 reduce-scatter.1
  152.7 36.6 all-reduce.4
  191.8 28.5 all-reduce.2
